TPU v7x, 32 devices: a whole 2x2x4 slice. The times are simulated.
32 devices in a mesh: dp: 4 (over z), row: 4 (over y, x), col: 2 (over core).
Axes of the slice: x: 2, y: 2, z: 4, core: 2. Of those that a mesh axis runs over, the one named last changes fastest.
Arguments:
- tokens: bfloat16 [4096, 1, 960], P('dp', None, ('row', 'col')), may hold values from -6 to 6
- seg_ids: int32 [1, 4096], replicated, may hold values from 0 to 3, never falling along the last dimension, each value on 1 to 3072 neighbouring positions
- gain_one: float32 [960], P(('row', 'col')), may hold values from 0.5 to 1.5
- w_query: bfloat16 [960, 960], P('row', 'col'), may hold values from -0.1875 to 0.1875
- key_weight: bfloat16 [960, 320], P('row', 'col'), may hold values from -0.1875 to 0.1875
- value_weight: bfloat16 [960, 320], P('row', 'col'), may hold values from -0.1875 to 0.1875
- w_out: bfloat16 [960, 960], P('col', 'row'), may hold values from -0.75 to 0.75
- gain_two: float32 [960], P(('row', 'col')), may hold values from 0.5 to 1.5
- w_gate: bfloat16 [960, 2560], P('row', 'col'), may hold values from -0.1875 to 0.1875
- w_up: bfloat16 [960, 2560], P('row', 'col'), may hold values from -0.1875 to 0.1875
- w_down: bfloat16 [2560, 960], P('col', 'row'), may hold values from -0.125 to 0.125
- grad_out: bfloat16 [4096, 1, 960], P('dp', None, ('row', 'col')), may hold values from -6 to 6
Outputs:
- output: bfloat16 [4096, 1, 960], P('dp', None, ('row', 'col'))
- grad_tokens: float32 [4096, 1, 960], P('dp', None, ('row', 'col'))
- grad_gain_one: float32 [960], P(('row', 'col'))
- grad_w_query: float32 [960, 960], P('row', ('col', 'dp'))
- grad_w_key: float32 [960, 320], P('row', ('col', 'dp'))
- grad_w_value: float32 [960, 320], P('row', ('col', 'dp'))
- grad_w_out: float32 [960, 960], P(('col', 'dp'), 'row')
- grad_gain_two: float32 [960], P(('row', 'col'))
- grad_w_gate: float32 [960, 2560], P('row', ('col', 'dp'))
- grad_w_up: float32 [960, 2560], P('row', ('col', 'dp'))
- grad_w_down: float32 [2560, 960], P(('col', 'dp'), 'row')
Inputs may be any that keep to these rules, and one draw needn't show every extreme that they name: Each row of seg_ids numbers the documents of one sequence from 0 upward, never falling; no document is longer than 3072 positions, and one is exactly that long.
All inputs are finite; a program needn't handle non-finite values.
Results may differ from a plain program's by a relative error of at most 0.035.
Values may be sent and summed in bfloat16 or wider, within the bound.
A program may use at most 128 MiB of HBM per device.

v0:
```python
import math

import jax
import jax.numpy as jnp
from jax import lax
from jax.sharding import PartitionSpec as P

MODEL_WIDTH = 960
QUERY_HEADS = 15
KEY_VALUE_HEADS = 5
HEAD_SIZE = 64
DOCS = 4


EPSILON = 1e-05
ROPE_BASE = 100000.0
MASKED = -1e30


def positions(segment_labels):
    labels = jnp.arange(DOCS, dtype=jnp.int32)
    member = (segment_labels[:, :, None] == labels[None, None, :]).astype(jnp.int32)
    counts = jnp.sum(member, axis=1)
    starts = jnp.cumsum(counts, axis=1) - counts
    first_pos = jnp.sum(member * starts[:, None, :], axis=2)
    position_index = jnp.arange(segment_labels.shape[1], dtype=jnp.int32)
    return position_index[None, :] - first_pos


def apply_rotary(inputs, token_positions, direction):
    half_dim = inputs.shape[-1] // 2
    frequency = jnp.power(
        ROPE_BASE, -jnp.arange(half_dim, dtype=jnp.float32) * (2.0 / inputs.shape[-1])
    )
    angles = jnp.transpose(token_positions).astype(jnp.float32)[:, :, None, None] * frequency
    cosine = jnp.cos(angles)
    sine_part = jnp.sin(angles) * direction
    first_half = inputs[..., :half_dim]
    second_half = inputs[..., half_dim:]
    return jnp.concatenate(
        [
            first_half * cosine - second_half * sine_part,
            second_half * cosine + first_half * sine_part,
        ],
        axis=-1,
    )


def width_total(partial_value):
    return lax.psum(partial_value, ("row", "col"))


def feature_gather(shard_in):
    return lax.all_gather(shard_in, "col", axis=1, tiled=True)


def feature_total(partial_value):
    return lax.psum_scatter(
        partial_value.astype(jnp.bfloat16), "col", scatter_dimension=1, tiled=True
    ).astype(jnp.float32)


def token_total(term_fn, row_count):
    return lax.psum_scatter(
        term_fn(jnp.int32(0), row_count * lax.axis_size("row")).astype(jnp.bfloat16),
        "row",
        scatter_dimension=0,
        tiled=True,
    ).astype(jnp.float32)


def spread_heads(packed):
    return lax.all_to_all(packed, "col", split_axis=0, concat_axis=1, tiled=True)


def merge_heads(packed):
    return lax.all_to_all(packed, "col", split_axis=1, concat_axis=0, tiled=True)


def norm_forward(stream, gain_vec):
    totals = width_total(jnp.sum(stream * stream, axis=1))
    inverse = lax.rsqrt(totals / MODEL_WIDTH + EPSILON)
    return (inverse, (stream * inverse[:, None] * gain_vec).astype(jnp.bfloat16))


def norm_backward(stream, gain_vec, inverse, grad_norm):
    weighted = grad_norm * gain_vec
    inner_sum = width_total(jnp.sum(weighted * stream, axis=1))
    grad_stream = (
        inverse[:, None] * weighted
        - stream * (inverse * inverse * inverse * inner_sum / MODEL_WIDTH)[:, None]
    )
    grad_gain = jnp.sum(grad_norm * stream * inverse[:, None], axis=0)
    return (grad_stream, grad_gain)


def row_project(shard_in, matrix):
    return jnp.dot(
        lax.all_gather(shard_in, "row", axis=0, tiled=True),
        matrix,
        preferred_element_type=jnp.float32,
    )


def weight_side(values_in, grad_rows_all):
    return lax.dot_general(
        lax.all_gather(values_in, "row", axis=0, tiled=True),
        grad_rows_all,
        (((0,), (0,)), ((), ())),
        preferred_element_type=jnp.float32,
    )


def input_side(grad_shard, matrix, inputs_all):
    pieces = lax.all_gather(grad_shard, "row", axis=0, tiled=True)
    w_grad = lax.dot_general(
        inputs_all, pieces, (((0,), (0,)), ((), ())), preferred_element_type=jnp.float32
    )
    part_grad = lax.dot_general(
        pieces, matrix, (((1,), (1,)), ((), ())), preferred_element_type=jnp.float32
    )
    return (w_grad, part_grad)


def shards(
    tokens,
    seg_ids,
    gain_one,
    w_query,
    key_weight,
    value_weight,
    w_out,
    gain_two,
    w_gate,
    w_up,
    w_down,
    grad_out,
):
    local_len, sequence_total, width = tokens.shape
    all_rows = local_len * sequence_total
    col_size = lax.axis_size("col")
    quarter = all_rows // lax.axis_size("row")
    eighth = quarter // col_size
    local_positions = eighth // sequence_total
    heads_per_group = QUERY_HEADS // KEY_VALUE_HEADS
    score_scale = 1.0 / math.sqrt(HEAD_SIZE)
    stream = tokens.reshape(all_rows, width).astype(jnp.float32)
    inverse_one, normed_one = norm_forward(stream, gain_one)
    cols_one = feature_gather(normed_one)
    w_joined = jnp.concatenate([w_query, key_weight, value_weight], axis=1)

    def joined_rows(offset, amount):
        return jnp.dot(cols_one, w_joined, preferred_element_type=jnp.float32)

    joined = token_total(joined_rows, quarter).astype(jnp.bfloat16)
    head_rows = spread_heads(joined.reshape(quarter, 1, -1))
    query_cols = w_query.shape[1]
    key_cols = key_weight.shape[1]
    query_raw = head_rows[:, :, :query_cols].reshape(
        local_positions, sequence_total, QUERY_HEADS, HEAD_SIZE
    )
    key_unrotated = head_rows[:, :, query_cols : query_cols + key_cols].reshape(
        local_positions, sequence_total, KEY_VALUE_HEADS, HEAD_SIZE
    )
    value_here = head_rows[:, :, query_cols + key_cols :].reshape(
        local_positions, sequence_total, KEY_VALUE_HEADS * HEAD_SIZE
    )
    all_places = positions(seg_ids)
    first_pos = lax.axis_index(("dp", "row", "col")) * local_positions
    query_segs = lax.dynamic_slice_in_dim(seg_ids, first_pos, local_positions, 1)
    query_positions = lax.dynamic_slice_in_dim(all_places, first_pos, local_positions, 1)
    query_index = first_pos + jnp.arange(local_positions, dtype=jnp.int32)
    queries = (
        apply_rotary(query_raw.astype(jnp.float32), query_positions, 1.0)
        .astype(jnp.bfloat16)
        .reshape(local_positions, sequence_total, KEY_VALUE_HEADS, heads_per_group, HEAD_SIZE)
    )
    keys_here = (
        apply_rotary(key_unrotated.astype(jnp.float32), query_positions, 1.0)
        .astype(jnp.bfloat16)
        .reshape(local_positions, sequence_total, KEY_VALUE_HEADS * HEAD_SIZE)
    )
    keys_all, values_all = (
        lax.all_gather(keys_here, ("dp", "row", "col"), axis=0, tiled=True),
        lax.all_gather(value_here, ("dp", "row", "col"), axis=0, tiled=True),
    )
    full_len = keys_all.shape[0]
    key_block_rows = min(512, full_len)
    count_of_blocks = full_len // key_block_rows
    block_starts = jnp.arange(count_of_blocks, dtype=jnp.int32) * key_block_rows

    def split_blocks(flattened):
        return flattened.reshape(
            count_of_blocks, key_block_rows, sequence_total, KEY_VALUE_HEADS, HEAD_SIZE
        )

    def block_scores(offset, key_part):
        products = (
            jnp.einsum("qsgjd,ksgd->sgjqk", queries, key_part, preferred_element_type=jnp.float32)
            * score_scale
        )
        key_segs = lax.dynamic_slice_in_dim(seg_ids, offset, key_block_rows, 1)
        key_index = offset + jnp.arange(key_block_rows, dtype=jnp.int32)
        allowed = (query_segs[:, :, None] == key_segs[:, None, :]) & (
            key_index[None, None, :] <= query_index[None, :, None]
        )
        return jnp.where(allowed[:, None, None], products, MASKED)

    def gather_stats(running, inputs):
        highest, totals = running
        offset, key_part = inputs
        scores = block_scores(offset, key_part)
        raised = jnp.maximum(highest, jnp.max(scores, axis=-1))
        totals = totals * jnp.exp(highest - raised) + jnp.sum(
            jnp.exp(scores - raised[..., None]), axis=-1
        )
        return ((raised, totals), None)

    statistic_shape = (sequence_total, KEY_VALUE_HEADS, heads_per_group, local_positions)
    stats_init = (
        jnp.full(statistic_shape, MASKED, jnp.float32),
        jnp.zeros(statistic_shape, jnp.float32),
    )
    (highest, totals), unused = lax.scan(
        gather_stats, stats_init, (block_starts, split_blocks(keys_all))
    )
    log_total = highest + jnp.log(totals)

    def mix_values(running, inputs):
        offset, key_part, value_part = inputs
        probability = jnp.exp(block_scores(offset, key_part) - log_total[..., None]).astype(
            jnp.bfloat16
        )
        return (
            running
            + jnp.einsum(
                "sgjqk,ksgd->qsgjd", probability, value_part, preferred_element_type=jnp.float32
            ),
            None,
        )

    attended_starting = jnp.zeros(
        (local_positions, sequence_total, KEY_VALUE_HEADS, heads_per_group, HEAD_SIZE), jnp.float32
    )
    attended_output, unused = lax.scan(
        mix_values,
        attended_starting,
        (block_starts, split_blocks(keys_all), split_blocks(values_all)),
    )
    merged = merge_heads(
        attended_output.astype(jnp.bfloat16).reshape(eighth, col_size, -1)
    ).reshape(quarter, -1)
    middle = stream + feature_total(row_project(merged, w_out))
    inverse_two, normed_two = norm_forward(middle, gain_two)
    cols_two = feature_gather(normed_two)
    w_pair = jnp.concatenate([w_gate, w_up], axis=1)

    def pair_rows(offset, amount):
        return jnp.dot(cols_two, w_pair, preferred_element_type=jnp.float32)

    pair_sums = token_total(pair_rows, quarter)
    half_ff = w_gate.shape[1]
    gate_values = pair_sums[:, :half_ff]
    up_values = pair_sums[:, half_ff:]
    sigmoid_gate = jax.nn.sigmoid(gate_values)
    hidden = (gate_values * sigmoid_gate * up_values).astype(jnp.bfloat16)
    output = (
        (middle + feature_total(row_project(hidden, w_down)))
        .astype(jnp.bfloat16)
        .reshape(local_len, sequence_total, width)
    )
    grad_low = grad_out.reshape(all_rows, width)
    grad_cols = feature_gather(grad_low)
    grad_w_down = weight_side(hidden, grad_cols)

    def hidden_rows(offset, amount):
        return lax.dot_general(
            grad_cols, w_down, (((1,), (1,)), ((), ())), preferred_element_type=jnp.float32
        )

    grad_hidden = token_total(hidden_rows, quarter)
    grad_gate = grad_hidden * up_values * sigmoid_gate * (1.0 + gate_values * (1.0 - sigmoid_gate))
    grad_up = grad_hidden * gate_values * sigmoid_gate
    grad_pair = jnp.concatenate([grad_gate, grad_up], axis=1).astype(jnp.bfloat16)
    grad_w_pair, grad_cols_two = input_side(grad_pair, w_pair, cols_two)
    back_two, grad_gain_two = norm_backward(
        middle, gain_two, inverse_two, feature_total(grad_cols_two)
    )
    grad_middle = grad_low.astype(jnp.float32) + back_two
    middle_cols = feature_gather(grad_middle.astype(jnp.bfloat16))
    grad_w_out = weight_side(merged, middle_cols)

    def merged_rows(offset, amount):
        return lax.dot_general(
            middle_cols, w_out, (((1,), (1,)), ((), ())), preferred_element_type=jnp.float32
        )

    grad_merged = token_total(merged_rows, quarter).astype(jnp.bfloat16)
    grad_attended = spread_heads(grad_merged.reshape(quarter, 1, -1)).reshape(
        local_positions, sequence_total, KEY_VALUE_HEADS, heads_per_group, HEAD_SIZE
    )
    row_delta = jnp.transpose(
        jnp.sum(grad_attended.astype(jnp.float32) * attended_output, axis=-1), (1, 2, 3, 0)
    )

    def attend_back(grad_query, inputs):
        offset, key_part, value_part = inputs
        probability = jnp.exp(block_scores(offset, key_part) - log_total[..., None])
        grad_probs = jnp.einsum(
            "qsgjd,ksgd->sgjqk", grad_attended, value_part, preferred_element_type=jnp.float32
        )
        grad_scores = (probability * (grad_probs - row_delta[..., None])).astype(jnp.bfloat16)
        grad_query = (
            grad_query
            + jnp.einsum(
                "sgjqk,ksgd->qsgjd", grad_scores, key_part, preferred_element_type=jnp.float32
            )
            * score_scale
        )
        grad_key = (
            jnp.einsum(
                "sgjqk,qsgjd->ksgd", grad_scores, queries, preferred_element_type=jnp.float32
            )
            * score_scale
        )
        grad_value = jnp.einsum(
            "sgjqk,qsgjd->ksgd",
            probability.astype(jnp.bfloat16),
            grad_attended,
            preferred_element_type=jnp.float32,
        )
        return (grad_query, (grad_key, grad_value))

    grad_query, (key_grads, value_grads) = lax.scan(
        attend_back,
        jnp.zeros(queries.shape, jnp.float32),
        (block_starts, split_blocks(keys_all), split_blocks(values_all)),
    )
    key_flat = key_grads.reshape(full_len, sequence_total, -1)
    value_flat = value_grads.reshape(full_len, sequence_total, -1)
    key_gradient_rows, grad_values = (
        lax.psum_scatter(key_flat, ("dp", "row", "col"), scatter_dimension=0, tiled=True),
        lax.psum_scatter(value_flat, ("dp", "row", "col"), scatter_dimension=0, tiled=True),
    )
    query_back = apply_rotary(
        grad_query.reshape(local_positions, sequence_total, QUERY_HEADS, HEAD_SIZE),
        query_positions,
        -1.0,
    )
    key_backward = apply_rotary(
        key_gradient_rows.reshape(local_positions, sequence_total, KEY_VALUE_HEADS, HEAD_SIZE),
        query_positions,
        -1.0,
    )
    packed = jnp.concatenate(
        [
            query_back.reshape(eighth, col_size, -1),
            key_backward.reshape(eighth, col_size, -1),
            grad_values.reshape(eighth, col_size, -1),
        ],
        axis=2,
    ).astype(jnp.bfloat16)
    grad_joined = merge_heads(packed).reshape(quarter, -1)
    grad_w_joined, grad_cols_one = input_side(grad_joined, w_joined, cols_one)
    back_one, grad_gain_one = norm_backward(
        stream, gain_one, inverse_one, feature_total(grad_cols_one)
    )
    grad_tokens = (grad_middle + back_one).reshape(local_len, sequence_total, width)
    gain_one_sum, gain_two_sum = lax.psum((grad_gain_one, grad_gain_two), "dp")
    query_part = grad_w_joined[:, :query_cols]
    key_part_grad = grad_w_joined[:, query_cols : query_cols + key_cols]
    value_part_grad = grad_w_joined[:, query_cols + key_cols :]
    gate_part = grad_w_pair[:, :half_ff]
    up_part = grad_w_pair[:, half_ff:]
    query_sum, key_sum, value_sum, out_sum, gate_sum, up_sum, down_sum = (
        lax.psum_scatter(
            query_part.astype(jnp.bfloat16), "dp", scatter_dimension=1, tiled=True
        ).astype(jnp.float32),
        lax.psum_scatter(
            key_part_grad.astype(jnp.bfloat16), "dp", scatter_dimension=1, tiled=True
        ).astype(jnp.float32),
        lax.psum_scatter(
            value_part_grad.astype(jnp.bfloat16), "dp", scatter_dimension=1, tiled=True
        ).astype(jnp.float32),
        lax.psum_scatter(
            grad_w_out.astype(jnp.bfloat16), "dp", scatter_dimension=0, tiled=True
        ).astype(jnp.float32),
        lax.psum_scatter(
            gate_part.astype(jnp.bfloat16), "dp", scatter_dimension=1, tiled=True
        ).astype(jnp.float32),
        lax.psum_scatter(
            up_part.astype(jnp.bfloat16), "dp", scatter_dimension=1, tiled=True
        ).astype(jnp.float32),
        lax.psum_scatter(
            grad_w_down.astype(jnp.bfloat16), "dp", scatter_dimension=0, tiled=True
        ).astype(jnp.float32),
    )
    return (
        output,
        grad_tokens,
        gain_one_sum,
        query_sum,
        key_sum,
        value_sum,
        out_sum,
        gain_two_sum,
        gate_sum,
        up_sum,
        down_sum,
    )


def solution(mesh):
    in_specs = (
        P("dp", None, ("row", "col")),
        P(),
        P(("row", "col")),
        P("row", "col"),
        P("row", "col"),
        P("row", "col"),
        P("col", "row"),
        P(("row", "col")),
        P("row", "col"),
        P("row", "col"),
        P("col", "row"),
        P("dp", None, ("row", "col")),
    )
    out_specs = (
        P("dp", None, ("row", "col")),
        P("dp", None, ("row", "col")),
        P(("row", "col")),
        P("row", ("col", "dp")),
        P("row", ("col", "dp")),
        P("row", ("col", "dp")),
        P(("col", "dp"), "row"),
        P(("row", "col")),
        P("row", ("col", "dp")),
        P("row", ("col", "dp")),
        P(("col", "dp"), "row"),
    )
    return jax.shard_map(shards, mesh=mesh, in_specs=in_specs, out_specs=out_specs, check_vma=False)
```

profile of v0, /device:TPU:0, one launch (start us, length us, event | category | flops | bytes accessed | tf_op | source)
XLA Modules:
  0.0 1473.5 jit_solution(13176449230874918196)
XLA Ops:
  8.3 15.1 %psum.42 = f32[1024]{0:T(1024)S(1)} all-reduce(f32[1024]{0:T(1024)S(1)} %fusion.101), channel_id=1, replica_groups=mesh['dp'=4,'row'=4,'col'=2] {'row','col'}, use_global_device_ids=true, to_apply=%region_1.0 | all-reduce | flops 1024 | bytes 8192 | tf_op jit(solution)/shard_map/psum | solution.py:50
  31.9 30.9 %reduce-scatter.22.cloned.1.call-done = bf16[256,800]{0,1:T(8,128)(2,1)} async-done(((bf16[1024,800]{0,1:T(8,128)(2,1)}), bf16[256,800]{0,1:T(8,128)(2,1)}) %reduce-scatter.22.cloned.1.call-update) | async-done | bytes 409616 | tf_op jit(solution)/shard_map/reduce_scatter | solution.py:64
  74.0 54.7 %all-gather.7.cloned.1.call-done = bf16[4096,1,320]{0,2,1:T(8,128)(2,1)} async-done(((bf16[128,1,320]{0,2,1:T(8,128)(2,1)}), bf16[4096,1,320]{0,2,1:T(8,128)(2,1)}) %all-gather.7.cloned.1.call-update) | async-done | bytes 2621456 | tf_op jit(solution)/shard_map/all_gather | solution.py:185
  134.1 52.9 %all-gather.9.cloned.1.call-done = bf16[4096,1,320]{0,2,1:T(8,128)(2,1)} async-done(((bf16[128,1,320]{0,2,1:T(8,128)(2,1)}), bf16[4096,1,320]{0,2,1:T(8,128)(2,1)}) %all-gather.9.cloned.1.call-update) | async-done | bytes 2621456 | tf_op jit(solution)/shard_map/all_gather | solution.py:184
  192.4 48.9 %while.39 = (s32[]{:T(128)}, f32[1,5,3,128]{3,2,1,0:T(4,128)S(1)}, f32[1,5,3,128]{3,2,1,0:T(4,128)S(1)}, s32[1,128]{1,0:T(1,128)S(1)}, s32[8]{0:T(128)S(1)}, /*i...) while((s32[]{:T(128)}, f32[1,5,3,128]{3,2,1,0:T(4,128)S(1)}, ...), condition=%wide.region_9.10_spmd.clone, body=%wide.region_6.9_spmd.clone.sunk | while | flops 132917248 | bytes 8746182 | solution.py:224
  241.4 48.1 %while.40 = (s32[]{:T(128)}, f32[128,1,5,3,64]{0,4,3,2,1:T(8,128)S(1)}, bf16[8,512,1,5,64]{1,4,3,2,0:T(8,128)(2,1)}, s32[1,128]{1,0:T(1,128)S(1)}, s32[8]{0:T(12...) while((s32[]{:T(128)}, ...), condition=%wide.region_11.12_spmd.clone, body=%wide.region_10.11_spmd.clone.sunk | while | flops 256033408 | bytes 2036424 | solution.py:245
  293.9 21.7 %all_gather.35 = bf16[1024,480]{0,1:T(8,128)(2,1)S(1)} all-gather(bf16[256,480]{0,1:T(8,128)(2,1)S(1)} %bitcast.423), channel_id=1, replica_groups=mesh['dp'=4,'row'=4,'col'=2] {'row'}, dimensions={0}, use_global_device_ids=true | all-gather | bytes 1228800 | tf_op jit(solution)/shard_map/all_gather | solution.py:99
  325.1 14.3 psum.43
  353.8 54.2 %reduce-scatter.26.cloned.1.call-done = bf16[256,2560]{1,0:T(8,128)(2,1)} async-done(((bf16[1024,2560]{1,0:T(8,128)(2,1)}), bf16[256,2560]{1,0:T(8,128)(2,1)}) %reduce-scatter.26.cloned.1.call-update) | async-done | bytes 1310736 | tf_op jit(solution)/shard_map/reduce_scatter | solution.py:64
  411.2 39.3 %reduce-scatter.30.cloned.1.call-done = bf16[256,1280]{1,0:T(8,128)(2,1)} async-done(((bf16[1024,1280]{1,0:T(8,128)(2,1)}), bf16[256,1280]{1,0:T(8,128)(2,1)}) %reduce-scatter.30.cloned.1.call-update) | async-done | bytes 655376 | tf_op jit(solution)/shard_map/reduce_scatter | solution.py:64
  455.2 61.5 %all-gather.13.cloned.1.call-done = bf16[1024,2560]{1,0:T(8,128)(2,1)} async-done(((bf16[256,2560]{1,0:T(8,128)(2,1)}), bf16[1024,2560]{1,0:T(8,128)(2,1)}) %all-gather.13.cloned.1.call-update) | async-done | bytes 5242896 | tf_op jit(solution)/shard_map/all_gather | solution.py:115
  516.7 4.8 convolution_convert_fusion.6
  521.6 8.0 reduce-scatter.32.cloned.1.call-done
  530.9 14.3 psum.44
  550.0 26.4 %reduce-scatter.34.cloned.1.call-done = bf16[256,480]{0,1:T(8,128)(2,1)} async-done(((bf16[1024,480]{0,1:T(8,128)(2,1)}), bf16[256,480]{0,1:T(8,128)(2,1)}) %reduce-scatter.34.cloned.1.call-update) | async-done | bytes 245776 | tf_op jit(solution)/shard_map/reduce_scatter | solution.py:64
  585.3 330.6 %while.41 = (s32[]{:T(128)}, f32[128,1,5,3,64]{0,4,3,2,1:T(8,128)S(1)}, f32[8,512,1,5,64]{1,0,4,3,2:T(8,128)}, f32[8,512,1,5,64]{1,0,4,3,2:T(8,128)}, bf16[8,512...) while((s32[]{:T(128)}, ...), condition=%wide.region_24.25_spmd.clone, body=%wide.region_23.24_spmd.clone.sunk | while | flops 639705728 | bytes 27429116 | solution.py:334
  598.5 14.1 dynamic_update_slice.11
  612.6 14.1 dynamic_update_slice.12
  639.8 14.1 dynamic_update_slice.11
  653.9 14.1 dynamic_update_slice.12
  681.1 14.1 dynamic_update_slice.11
  695.2 14.1 dynamic_update_slice.12
  722.4 14.1 dynamic_update_slice.11
  736.5 14.1 dynamic_update_slice.12
  763.8 14.1 dynamic_update_slice.11
  777.8 14.1 dynamic_update_slice.12
  805.1 14.1 dynamic_update_slice.11
  819.2 14.1 dynamic_update_slice.12
  846.4 14.1 dynamic_update_slice.11
  860.5 14.1 dynamic_update_slice.12
  887.7 14.1 dynamic_update_slice.11
  901.8 14.1 dynamic_update_slice.12
  915.9 6.8 reshape.813
  922.8 6.8 reshape.810
  930.4 135.7 %reduce-scatter.38.cloned.1.call-done = f32[128,1,320]{0,2,1:T(8,128)} async-done(((f32[4096,1,320]{0,2,1:T(8,128)}), f32[128,1,320]{0,2,1:T(8,128)}) %reduce-scatter.38.cloned.1.call-update) | async-done | bytes 163856 | tf_op jit(solution)/shard_map/reduce_scatter | solution.py:343
  1067.0 140.4 %reduce-scatter.36.cloned.1.call-done = f32[128,1,320]{0,2,1:T(8,128)} async-done(((f32[4096,1,320]{0,2,1:T(8,128)}), f32[128,1,320]{0,2,1:T(8,128)}) %reduce-scatter.36.cloned.1.call-update) | async-done | bytes 163856 | tf_op jit(solution)/shard_map/reduce_scatter | solution.py:342
  1213.7 31.0 %all-gather.11.cloned.1.call-done = bf16[1024,1280]{1,0:T(8,128)(2,1)} async-done(((bf16[256,1280]{1,0:T(8,128)(2,1)}), bf16[1024,1280]{1,0:T(8,128)(2,1)}) %all-gather.11.cloned.1.call-update) | async-done | bytes 2621456 | tf_op jit(solution)/shard_map/all_gather | solution.py:99
  1257.1 20.8 %all-gather.15.cloned.1.call-done = bf16[1024,800]{0,1:T(8,128)(2,1)} async-done(((bf16[256,800]{0,1:T(8,128)(2,1)}), bf16[1024,800]{0,1:T(8,128)(2,1)}) %all-gather.15.cloned.1.call-update) | async-done | bytes 1638416 | tf_op jit(solution)/shard_map/all_gather | solution.py:115
  1288.8 13.4 reduce-scatter.50.cloned.1.call-done
  1303.9 21.5 %reduce-scatter.54.cloned.1.call-done = bf16[320,240]{1,0:T(8,128)(2,1)} async-done(((bf16[1280,240]{1,0:T(8,128)(2,1)}), bf16[320,240]{1,0:T(8,128)(2,1)}) %reduce-scatter.54.cloned.1.call-update) | async-done | bytes 153616
  1327.4 21.3 %reduce-scatter.52.cloned.1.call-done = bf16[320,240]{1,0:T(8,128)(2,1)} async-done(((bf16[1280,240]{1,0:T(8,128)(2,1)}), bf16[320,240]{1,0:T(8,128)(2,1)}) %reduce-scatter.52.cloned.1.call-update) | async-done | bytes 153616
  1350.6 18.7 %reduce-scatter.48.cloned.1.call-done = bf16[120,240]{1,0:T(8,128)(2,1)} async-done(((bf16[480,240]{1,0:T(8,128)(2,1)}), bf16[120,240]{1,0:T(8,128)(2,1)}) %reduce-scatter.48.cloned.1.call-update) | async-done | bytes 57616 | tf_op jit(solution)/shard_map/reduce_scatter | solution.py:385
  1370.8 18.1 %reduce-scatter.44.cloned.1.call-done = bf16[240,40]{0,1:T(8,128)(2,1)} async-done(((bf16[240,160]{0,1:T(8,128)(2,1)}), bf16[240,40]{0,1:T(8,128)(2,1)}) %reduce-scatter.44.cloned.1.call-update) | async-done | bytes 19216 | tf_op jit(solution)/shard_map/reduce_scatter | solution.py:379
  1390.2 18.8 %reduce-scatter.46.cloned.1.call-done = bf16[240,40]{0,1:T(8,128)(2,1)} async-done(((bf16[240,160]{0,1:T(8,128)(2,1)}), bf16[240,40]{0,1:T(8,128)(2,1)}) %reduce-scatter.46.cloned.1.call-update) | async-done | bytes 19216 | tf_op jit(solution)/shard_map/reduce_scatter | solution.py:382
  1410.3 19.3 %reduce-scatter.42.cloned.1.call-done = bf16[240,120]{0,1:T(8,128)(2,1)} async-done(((bf16[240,480]{0,1:T(8,128)(2,1)}), bf16[240,120]{0,1:T(8,128)(2,1)}) %reduce-scatter.42.cloned.1.call-update) | async-done | bytes 57616 | tf_op jit(solution)/shard_map/reduce_scatter | solution.py:376
  1431.2 7.4 reduce-scatter.40.cloned.1.call-done
  1439.8 12.4 all-reduce
  1452.3 12.1 psum.45
  (422 shorter events, 282.3 us)
Async XLA Ops:
  7.2 344.0 %copy-start = (bf16[1280,240]{0,1:T(8,128)(2,1)S(1)}, bf16[1280,240]{0,1:T(8,128)(2,1)}, u32[]{:S(2)}) copy-start(bf16[1280,240]{0,1:T(8,128)(2,1)} %param.28) | copy-start | bytes 1843204
  7.2 55.6 %reduce-scatter.22.cloned.1.call-start = ((), (), s32[]{:S(2)}) async-start(), calls=%async_computation.21 | async-start | bytes 2048000 | tf_op jit(solution)/shard_map/reduce_scatter | solution.py:64
  25.4 6.4 copy-start.17
  28.7 36.8 %copy-start.12 = (bf16[1024,240]{0,1:T(8,128)(2,1)}, bf16[1024,240]{0,1:T(8,128)(2,1)S(1)}, u32[]{:S(2)}) copy-start(bf16[1024,240]{0,1:T(8,128)(2,1)S(1)} %all_gather.32) | copy-start | bytes 1474564
  31.8 96.9 %all-gather.7.cloned.1.call-start = ((), (), s32[]{:S(2)}) async-start(), calls=%async_computation.22 | async-start | bytes 2703360 | tf_op jit(solution)/shard_map/all_gather | solution.py:185
  66.3 6.1 copy-start.19
  72.3 114.7 %all-gather.9.cloned.1.call-start = ((), (), s32[]{:S(2)}) async-start(), calls=%async_computation.23 | async-start | bytes 2703360 | tf_op jit(solution)/shard_map/all_gather | solution.py:184
  73.8 250.2 %reduce-scatter.24.cloned.1.call-start = ((), (), s32[]{:S(2)}) async-start(), calls=%async_computation.24 | async-start | bytes 737280 | tf_op jit(solution)/shard_map/reduce_scatter | solution.py:58
  289.5 27.0 %copy-start.15 = (bf16[480,240]{1,0:T(8,128)(2,1)S(1)}, bf16[480,240]{1,0:T(8,128)(2,1)}, u32[]{:S(2)}) copy-start(bf16[480,240]{1,0:T(8,128)(2,1)} %param.24) | copy-start | bytes 691204
  315.6 0.9 copy-start.3
  316.5 7.5 copy-start.1
  316.5 22.9 %copy-start.21 = (f32[120]{0:T(128)S(1)}, f32[120]{0:T(128)}, u32[]{:S(2)}) copy-start(f32[120]{0:T(128)} %param.25) | copy-start | bytes 1444
  317.8 90.2 %reduce-scatter.26.cloned.1.call-start = ((), (), s32[]{:S(2)}) async-start(), calls=%async_computation.25 | async-start | bytes 6553600 | tf_op jit(solution)/shard_map/reduce_scatter | solution.py:64
  342.6 0.8 copy-start.7
  347.3 0.9 copy-start.9
  347.3 103.1 %reduce-scatter.30.cloned.1.call-start = ((), (), s32[]{:S(2)}) async-start(), calls=%async_computation.28 | async-start | bytes 3276800 | tf_op jit(solution)/shard_map/reduce_scatter | solution.py:64
  350.4 0.8 copy-start.5
  353.8 163.0 %all-gather.13.cloned.1.call-start = ((), (), s32[]{:S(2)}) async-start(), calls=%async_computation.29 | async-start | bytes 6553600 | tf_op jit(solution)/shard_map/all_gather | solution.py:115
  455.2 74.5 %copy-start.2 = (bf16[1024,120]{0,1:T(8,128)(2,1)S(1)}, bf16[1024,120]{0,1:T(8,128)(2,1)}, u32[]{:S(2)}) copy-start(bf16[1024,120]{0,1:T(8,128)(2,1)} %reduce-scatter.24.cloned.1.call-done) | copy-start | bytes 737284
  455.2 74.5 %reduce-scatter.32.cloned.1.call-start = ((), (), s32[]{:S(2)}) async-start(), calls=%async_computation.30 | async-start | bytes 737280 | tf_op jit(solution)/shard_map/reduce_scatter | solution.py:58
  521.5 27.0 %copy-start.16 = (bf16[480,240]{1,0:T(8,128)(2,1)S(1)}, bf16[480,240]{1,0:T(8,128)(2,1)}, u32[]{:S(2)}) copy-start(bf16[480,240]{1,0:T(8,128)(2,1)} %param.24) | copy-start | bytes 691204
  521.6 54.9 %reduce-scatter.34.cloned.1.call-start = ((), (), s32[]{:S(2)}) async-start(), calls=%async_computation.31 | async-start | bytes 1228800 | tf_op jit(solution)/shard_map/reduce_scatter | solution.py:64
  548.5 1.5 copy-start.14
  550.0 516.1 %reduce-scatter.38.cloned.1.call-start = ((), (), s32[]{:S(2)}) async-start(), calls=%async_computation.33 | async-start | bytes 5406720 | tf_op jit(solution)/shard_map/reduce_scatter | solution.py:343
  922.7 284.7 %reduce-scatter.36.cloned.1.call-start = ((), (), s32[]{:S(2)}) async-start(), calls=%async_computation.32 | async-start | bytes 5406720 | tf_op jit(solution)/shard_map/reduce_scatter | solution.py:342
  929.6 315.1 %all-gather.11.cloned.1.call-start = ((), (), s32[]{:S(2)}) async-start(), calls=%async_computation.26 | async-start | bytes 3276800 | tf_op jit(solution)/shard_map/all_gather | solution.py:99
  930.2 347.7 %all-gather.15.cloned.1.call-start = ((), (), s32[]{:S(2)}) async-start(), calls=%async_computation.34 | async-start | bytes 2048000 | tf_op jit(solution)/shard_map/all_gather | solution.py:115
  930.3 314.3 %copy-start.6 = (bf16[1024,1,240]{0,2,1:T(8,128)(2,1)S(1)}, bf16[1024,1,240]{0,2,1:T(8,128)(2,1)}, u32[]{:S(2)}) copy-start(bf16[1024,1,240]{0,2,1:T(8,128)(2,1)} %copy-done.5) | copy-start | bytes 1474564
  1213.6 34.6 %copy-start.8 = (bf16[1024,240]{0,1:T(8,128)(2,1)S(1)}, bf16[1024,240]{0,1:T(8,128)(2,1)}, u32[]{:S(2)}) copy-start(bf16[1024,240]{0,1:T(8,128)(2,1)} %copy-done.7) | copy-start | bytes 1474564
  1213.6 88.6 %reduce-scatter.50.cloned.1.call-start = ((), (), s32[]{:S(2)}) async-start(), calls=%async_computation.40 | async-start | bytes 819200 | tf_op jit(solution)/shard_map/reduce_scatter | solution.py:394
  1248.2 77.2 %reduce-scatter.54.cloned.1.call-start = ((), (), s32[]{:S(2)}) async-start(), calls=%async_computation.42 | async-start | bytes 819200
  1252.2 2.5 copy-start.4
  1253.4 24.5 %copy-start.13 = (bf16[1024,240]{0,1:T(8,128)(2,1)S(1)}, bf16[1024,240]{0,1:T(8,128)(2,1)}, u32[]{:S(2)}) copy-start(bf16[1024,240]{0,1:T(8,128)(2,1)} %copy-done.12) | copy-start | bytes 1474564
  1253.5 95.2 %reduce-scatter.52.cloned.1.call-start = ((), (), s32[]{:S(2)}) async-start(), calls=%async_computation.41 | async-start | bytes 819200
  1254.6 27.6 %copy-start.18 = (bf16[240,160]{1,0:T(8,128)(2,1)S(1)}, bf16[240,160]{1,0:T(8,128)(2,1)}, u32[]{:S(2)}) copy-start(bf16[240,160]{1,0:T(8,128)(2,1)} %copy-done.17) | copy-start | bytes 230404
  1254.6 27.6 %copy-start.20 = (bf16[240,480]{1,0:T(8,128)(2,1)S(1)}, bf16[240,480]{1,0:T(8,128)(2,1)}, u32[]{:S(2)}) copy-start(bf16[240,480]{1,0:T(8,128)(2,1)} %param.21) | copy-start | bytes 691204
  1254.6 114.7 %reduce-scatter.48.cloned.1.call-start = ((), (), s32[]{:S(2)}) async-start(), calls=%async_computation.39 | async-start | bytes 307200 | tf_op jit(solution)/shard_map/reduce_scatter | solution.py:385
  1257.0 131.8 %reduce-scatter.44.cloned.1.call-start = ((), (), s32[]{:S(2)}) async-start(), calls=%async_computation.37 | async-start | bytes 102400 | tf_op jit(solution)/shard_map/reduce_scatter | solution.py:379
  1280.7 128.3 %reduce-scatter.46.cloned.1.call-start = ((), (), s32[]{:S(2)}) async-start(), calls=%async_computation.38 | async-start | bytes 102400 | tf_op jit(solution)/shard_map/reduce_scatter | solution.py:382
  1281.4 148.2 %reduce-scatter.42.cloned.1.call-start = ((), (), s32[]{:S(2)}) async-start(), calls=%async_computation.36 | async-start | bytes 307200 | tf_op jit(solution)/shard_map/reduce_scatter | solution.py:376
  1282.2 156.4 %reduce-scatter.40.cloned.1.call-start = ((), (), s32[]{:S(2)}) async-start(), calls=%async_computation.35 | async-start | bytes 737280 | tf_op jit(solution)/shard_map/reduce_scatter | solution.py:58
  1285.2 179.2 %reduce-scatter.28.cloned.1.call-start = ((), (), s32[]{:S(2)}) async-start(), calls=%async_computation.27 | async-start | bytes 737280 | tf_op jit(solution)/shard_map/reduce_scatter | solution.py:58
  1288.8 149.8 %copy-start.22 = (f32[120]{0:T(128)S(1)}, f32[120]{0:T(128)}, u32[]{:S(2)}) copy-start(f32[120]{0:T(128)} %param.20) | copy-start | bytes 1444
  1288.8 175.6 %copy-start.10 = (bf16[1024,1,120]{0,2,1:T(8,128)(2,1)S(1)}, bf16[1024,1,120]{0,2,1:T(8,128)(2,1)}, u32[]{:S(2)}) copy-start(bf16[1024,1,120]{0,2,1:T(8,128)(2,1)} %param.29) | copy-start | bytes 737284
  1288.8 175.6 %copy-start.11 = (bf16[1024,120]{0,1:T(8,128)(2,1)S(1)}, bf16[1024,120]{0,1:T(8,128)(2,1)}, u32[]{:S(2)}) copy-start(bf16[1024,120]{0,1:T(8,128)(2,1)} %reduce-scatter.32.cloned.1.call-done) | copy-start | bytes 737284
Sparse Core Ops, SparseCore 0:
  32.0 30.7 reduce-scatter.21
  72.4 56.2 all-gather.6
  132.2 54.7 all-gather.8
  317.9 6.0 reduce-scatter.23
  347.4 60.5 reduce-scatter.25
  410.9 39.5 reduce-scatter.29
  455.3 61.4 all-gather.12
  521.7 7.9 reduce-scatter.31
  550.1 26.3 reduce-scatter.33
  922.8 143.1 reduce-scatter.37
  1068.4 138.9 reduce-scatter.35
  1209.1 35.5 all-gather.10
  1246.5 31.3 all-gather.14
  1280.0 22.1 reduce-scatter.49
  1304.4 21.0 reduce-scatter.53
  1327.6 21.0 reduce-scatter.51
  1350.8 18.5 reduce-scatter.47
  1371.5 17.3 reduce-scatter.43
  1391.7 17.2 reduce-scatter.45
  1411.7 17.7 reduce-scatter.41
  1432.4 6.1 reduce-scatter.39
  1440.9 9.0 reduce-scatter.27
where the time goes:
time: 1480 us; the launch traced here: 1470 us
  waiting for transfers between devices  800 us (54%)
  local copies, waits for them, and re-layouts  300 us (20%)
  matrix products  135 us (9%)
  blocking collectives  115 us (8%)
  other arithmetic  59.3 us (4%)
  loops' own time  48.1 us (3%)
  between operations  15 us (1%)
    dynamic_update_slice x32, local copies, waits for them, and re-layouts, shards(): lax.scan(attend_back, jnp.zeros(queries.shape, jnp.float32), (block_start...  236 us
    reduce_scatter x4, waiting for transfers between devices, token_total(): lax.psum_scatter(term_fn(jnp.int32(0), row_count * lax.axis_size('row'))....  151 us
    reduce_scatter x1, waiting for transfers between devices, shards(): lax.psum_scatter(key_flat, ('dp', 'row', 'col'), scatter_dimension=0, til...  140 us
    reduce_scatter x1, waiting for transfers between devices, shards(): lax.psum_scatter(value_flat, ('dp', 'row', 'col'), scatter_dimension=0, t...  136 us
    all_gather x2, waiting for transfers between devices, input_side(): pieces = lax.all_gather(grad_shard, 'row', axis=0, tiled=True)  82.3 us
    psum x4, blocking collectives, width_total(): return lax.psum(partial_value, ('row', 'col'))  55.8 us
    all_gather x1, waiting for transfers between devices, shards(): lax.all_gather(value_here, ('dp', 'row', 'col'), axis=0, tiled=True)  54.7 us
    all_gather x1, waiting for transfers between devices, shards(): lax.all_gather(keys_here, ('dp', 'row', 'col'), axis=0, tiled=True)  52.9 us
  transfers between devices with their start and end apart: 22, of which 21 were waited for; matrix products, arithmetic and copies ran while one was open for 4% of the time, Pallas kernels for 0%

commit v1 on v0

v1 whole, which is shorter than its diff:
```python
import functools
import math

import jax
import jax.numpy as jnp
from jax import lax
from jax.experimental import pallas as pl
from jax.experimental.pallas import tpu as pltpu
from jax.sharding import PartitionSpec as P

MODEL_WIDTH = 960
QUERY_HEADS = 15
KEY_VALUE_HEADS = 5
HEAD_SIZE = 64
GROUP = QUERY_HEADS // KEY_VALUE_HEADS
DOCS = 4
EPSILON = 1e-05
ROPE_BASE = 100000.0
MASKED = -1e30
MESH = pl.DeviceIdType.MESH
F32 = jnp.float32
BF16 = jnp.bfloat16


def positions_start(segment_labels):
    labels = jnp.arange(DOCS, dtype=jnp.int32)
    member = (segment_labels[:, :, None] == labels[None, None, :]).astype(jnp.int32)
    counts = jnp.sum(member, axis=1)
    starts = jnp.cumsum(counts, axis=1) - counts
    return jnp.sum(member * starts[:, None, :], axis=2)[0]


def rotary(inputs, cosine, sine):
    first_half = inputs[..., :32]
    second_half = inputs[..., 32:]
    return jnp.concatenate(
        [
            first_half * cosine - second_half * sine,
            second_half * cosine + first_half * sine,
        ],
        axis=-1,
    )


def exchange_kernel(axes, sizes, modes, offsets, counts, *refs):
    k = len(modes)
    ins, outs = refs[:k], refs[k : 2 * k]
    send, recv, local = refs[2 * k :]
    here = [lax.axis_index(a) for a in axes]

    def source(i, place):
        how, span = modes[i]
        if how == "whole":
            return ins[i]
        if how == "lead":
            return ins[i].at[place[0]]
        return ins[i].at[tuple(place[:span])]

    barrier = pltpu.get_barrier_semaphore()
    places = []
    for off in offsets:
        place = [lax.rem(h + o, s) for h, o, s in zip(here, off, sizes)]
        places.append(place)
        pl.semaphore_signal(
            barrier, inc=1, device_id=dict(zip(axes, place)), device_id_type=MESH
        )
    pl.semaphore_wait(barrier, len(offsets))
    copies = []
    slot = 0
    for off, place in zip(offsets, places):
        for i, (how, span) in enumerate(modes):
            if any(off[span:]):
                continue
            copy = pltpu.make_async_remote_copy(
                src_ref=source(i, place),
                dst_ref=outs[i].at[tuple(here[:span])],
                send_sem=send.at[slot],
                recv_sem=recv.at[slot],
                device_id=dict(zip(axes, place)),
                device_id_type=MESH,
            )
            copy.start()
            copies.append(copy)
            slot += 1
    for i, (how, span) in enumerate(modes):
        copy = pltpu.make_async_copy(
            source(i, here), outs[i].at[tuple(here[:span])], local.at[i]
        )
        copy.start()
        copies.append(copy)
    for copy in copies:
        copy.wait()


def exchange(number, axes, parts):
    sizes = [lax.axis_size(a) for a in axes]
    offsets = [()]
    for s in sizes:
        offsets = [o + (j,) for o in offsets for j in range(s)]
    offsets = [o for o in offsets if any(o)]
    modes = [(how, span) for how, span, _ in parts]
    arrays = [a for _, _, a in parts]
    shapes = []
    for how, span, a in parts:
        lead = {"whole": 0, "lead": 1, "block": span}[how]
        shapes.append(jax.ShapeDtypeStruct(tuple(sizes[:span]) + a.shape[lead:], a.dtype))
    slots = sum(1 for o in offsets for _, span in modes if not any(o[span:]))
    any_spec = pl.BlockSpec(memory_space=pl.ANY)
    return pl.pallas_call(
        functools.partial(exchange_kernel, axes, sizes, modes, offsets, None),
        out_shape=shapes,
        in_specs=[any_spec] * len(arrays),
        out_specs=[any_spec] * len(arrays),
        scratch_shapes=[
            pltpu.SemaphoreType.DMA((slots,)),
            pltpu.SemaphoreType.DMA((slots,)),
            pltpu.SemaphoreType.DMA((len(arrays),)),
        ],
        compiler_params=pltpu.CompilerParams(collective_id=number, has_side_effects=True),
        name="exchange_%d" % number,
    )(*arrays)


def dot(a, b, ca, cb):
    return lax.dot_general(a, b, (((ca,), (cb,)), ((), ())), preferred_element_type=F32)


def block_mask(step, block, lo_ref, hi_ref, rows):
    index = step * block + lax.broadcasted_iota(jnp.int32, (rows, block), 1)
    return (index >= lo_ref[...]) & (index <= hi_ref[...])


def forward_kernel(block, span_ref, q_ref, kv_ref, lo_ref, hi_ref, o_ref, lse_ref):
    rows = q_ref.shape[1]
    q = q_ref[0]

    def step(j, carry):
        high, total, acc = carry
        kv = kv_ref[pl.ds(pl.multiple_of(j * block, block), block), :]
        ok = block_mask(j, block, lo_ref, hi_ref, rows)
        scores = jnp.where(ok, dot(q, kv, 1, 1), MASKED)
        raised = jnp.maximum(high, jnp.max(scores, axis=1, keepdims=True))
        weight = jnp.exp(scores - raised)
        scale = jnp.exp(high - raised)
        total = total * scale + jnp.sum(weight, axis=1, keepdims=True)
        acc = acc * scale + dot(weight.astype(BF16), kv, 1, 0)
        return raised, total, acc

    init = (
        jnp.full((rows, 1), MASKED, F32),
        jnp.zeros((rows, 1), F32),
        jnp.zeros((rows, 128), F32),
    )
    high, total, acc = lax.fori_loop(span_ref[0], span_ref[1], step, init)
    o_ref[0] = acc / total
    lse_ref[0] = high + jnp.log(total)


def backward_kernel(
    block, span_ref, q_ref, do_ref, kv_ref, lo_ref, hi_ref, lse_ref, delta_ref, dq_ref, dkv_ref
):
    rows = q_ref.shape[1]
    q = q_ref[0]
    do = do_ref[0]
    lse = lse_ref[0]
    delta = delta_ref[0]
    dkv_ref[...] = jnp.zeros_like(dkv_ref)

    def step(j, acc):
        at = pl.ds(pl.multiple_of(j * block, block), block)
        kv = kv_ref[at, :]
        ok = block_mask(j, block, lo_ref, hi_ref, rows)
        scores = jnp.where(ok, dot(q, kv, 1, 1), MASKED)
        prob = jnp.exp(scores - lse)
        gs = (prob * (dot(do, kv, 1, 1) - delta)).astype(BF16)
        dkv_ref[at, :] = (dot(gs, q, 0, 0) + dot(prob.astype(BF16), do, 0, 0)).astype(BF16)
        return acc + dot(gs, kv, 1, 0)

    dq_ref[0] = lax.fori_loop(
        span_ref[0], span_ref[1], step, jnp.zeros((rows, 128), F32)
    )


def attention_specs(rows, length):
    head = pl.BlockSpec((1, rows, 128), lambda g, s: (g, 0, 0))
    kv = pl.BlockSpec((length, 128), lambda g, s: (0, g))
    bound = pl.BlockSpec((rows, 1), lambda g, s: (0, 0))
    stat = pl.BlockSpec((1, rows, 1), lambda g, s: (g, 0, 0))
    return head, kv, bound, stat


def attention_forward(span, q, kv, lo, hi, block):
    heads, rows, _ = q.shape
    head, kvs, bound, stat = attention_specs(rows, kv.shape[0])
    return pl.pallas_call(
        functools.partial(forward_kernel, block),
        grid_spec=pltpu.PrefetchScalarGridSpec(
            num_scalar_prefetch=1,
            grid=(heads,),
            in_specs=[head, kvs, bound, bound],
            out_specs=[head, stat],
        ),
        out_shape=[
            jax.ShapeDtypeStruct((heads, rows, 128), F32),
            jax.ShapeDtypeStruct((heads, rows, 1), F32),
        ],
        compiler_params=pltpu.CompilerParams(vmem_limit_bytes=40 * 2**20),
        name="attend",
    )(span, q, kv, lo, hi)


def attention_backward(span, q, do, kv, lo, hi, lse, delta, block):
    heads, rows, _ = q.shape
    head, kvs, bound, stat = attention_specs(rows, kv.shape[0])
    return pl.pallas_call(
        functools.partial(backward_kernel, block),
        grid_spec=pltpu.PrefetchScalarGridSpec(
            num_scalar_prefetch=1,
            grid=(heads,),
            in_specs=[head, head, kvs, bound, bound, stat, stat],
            out_specs=[head, kvs],
        ),
        out_shape=[
            jax.ShapeDtypeStruct((heads, rows, 128), F32),
            jax.ShapeDtypeStruct(kv.shape, BF16),
        ],
        compiler_params=pltpu.CompilerParams(vmem_limit_bytes=40 * 2**20),
        name="attend_back",
    )(span, q, do, kv, lo, hi, lse, delta)


def norm(x, gain):
    inverse = lax.rsqrt(jnp.mean(x * x, axis=1, keepdims=True) + EPSILON)
    return inverse, (x * inverse * gain).astype(BF16)


def norm_back(x, gain, inverse, grad):
    weighted = grad * gain
    inner = jnp.sum(weighted * x, axis=1, keepdims=True)
    back = inverse * weighted - x * (inverse * inverse * inverse * inner / MODEL_WIDTH)
    return back, jnp.sum(grad * x * inverse, axis=0)


def pad8(v):
    return jnp.broadcast_to(v[None, :], (8,) + v.shape)


def total32(a, axis=0):
    return jnp.sum(a.astype(F32), axis=axis)


def shards(
    tokens,
    seg_ids,
    gain_one,
    w_query,
    key_weight,
    value_weight,
    w_out,
    gain_two,
    w_gate,
    w_up,
    w_down,
    grad_out,
):
    length, sequences, part = tokens.shape
    dps, rows, cols = (lax.axis_size(a) for a in ("dp", "row", "col"))
    chip_len = length // rows
    own = chip_len // cols
    col = lax.axis_index("col")
    qc, kc, half = w_query.shape[1], key_weight.shape[1], w_gate.shape[1]
    row_block = w_query.shape[0]
    width = row_block * rows

    pair_block = jnp.concatenate([w_gate, w_up], axis=1)
    w_pair = lax.all_gather(pair_block, "row", axis=0, tiled=True)
    w_down_half = lax.all_gather(w_down, "row", axis=1, tiled=True)

    joined_block = jnp.concatenate([w_query, key_weight, value_weight], axis=1)
    gains_in = jnp.concatenate([pad8(gain_one), pad8(gain_two)], axis=0)
    x_parts, g_parts, gain_parts, joined_rows, out_cols = exchange(
        0,
        ("row", "col"),
        [
            ("lead", 2, tokens.reshape(rows, chip_len, part)),
            ("lead", 2, grad_out.reshape(rows, chip_len, part)),
            ("whole", 2, gains_in),
            ("whole", 1, joined_block),
            ("whole", 1, w_out),
        ],
    )
    joined_all, out_all = exchange(
        1, ("col",), [("whole", 1, joined_rows), ("whole", 1, out_cols)]
    )
    w_joined = jnp.transpose(joined_all, (1, 2, 0, 3)).reshape(width, cols, -1)
    w_q = w_joined[:, :, :qc].reshape(width, cols * qc)
    w_k = w_joined[:, :, qc : qc + kc].reshape(width, cols * kc)
    w_v = w_joined[:, :, qc + kc :].reshape(width, cols * kc)
    w_qkv = jnp.concatenate([w_q, w_k, w_v], axis=1)
    w_o = jnp.transpose(out_all, (0, 2, 1, 3)).reshape(cols * w_out.shape[0], width)

    gain_parts = gain_parts.reshape(rows * cols, 2, 8, part)[:, :, 0]
    gain1 = gain_parts[:, 0].reshape(1, width)
    gain2 = gain_parts[:, 1].reshape(1, width)
    x_chip = jnp.transpose(x_parts, (2, 0, 1, 3)).reshape(chip_len, width).astype(F32)
    g_chip = jnp.transpose(g_parts, (2, 0, 1, 3)).reshape(chip_len, width)
    x_own = lax.dynamic_slice_in_dim(x_chip, col * own, own, 0)
    g_own = lax.dynamic_slice_in_dim(g_chip, col * own, own, 0).astype(F32)

    normed_one_chip = norm(x_chip, gain1)[1]
    inverse_one, normed_one = norm(x_own, gain1)
    qkv = dot(normed_one, w_qkv, 1, 0).astype(BF16).astype(F32)

    first_pos = lax.axis_index(("dp", "row", "col")) * own
    starts = positions_start(seg_ids)
    my_start = lax.dynamic_slice_in_dim(starts, first_pos, own, 0)
    my_index = first_pos + jnp.arange(own, dtype=jnp.int32)
    places = my_index - my_start
    frequency = jnp.power(ROPE_BASE, -jnp.arange(32, dtype=F32) * (2.0 / HEAD_SIZE))
    angles = places.astype(F32)[:, None, None] * frequency
    cosine, sine = jnp.cos(angles), jnp.sin(angles)
    nq, nk = QUERY_HEADS * HEAD_SIZE, KEY_VALUE_HEADS * HEAD_SIZE
    q = rotary(qkv[:, :nq].reshape(own, QUERY_HEADS, HEAD_SIZE), cosine, sine).astype(BF16)
    k = rotary(qkv[:, nq : nq + nk].reshape(own, KEY_VALUE_HEADS, HEAD_SIZE), cosine, sine)
    v = qkv[:, nq + nk :].reshape(own, KEY_VALUE_HEADS, HEAD_SIZE)
    kv = jnp.concatenate([k, v], axis=-1).astype(BF16).reshape(own, KEY_VALUE_HEADS * 128)

    (kv_dp,) = exchange(2, ("dp",), [("whole", 1, kv)])
    (kv_row,) = exchange(3, ("row",), [("whole", 1, kv_dp)])
    (kv_col,) = exchange(4, ("col",), [("whole", 1, kv_row)])
    full = own * dps * rows * cols
    kv_all = jnp.transpose(kv_col, (2, 1, 0, 3, 4)).reshape(full, KEY_VALUE_HEADS * 128)

    def to_heads(a):
        a = a.reshape(own, KEY_VALUE_HEADS, GROUP, HEAD_SIZE)
        return jnp.transpose(a, (1, 2, 0, 3)).reshape(KEY_VALUE_HEADS, GROUP * own, HEAD_SIZE)

    def from_heads(a):
        a = a.reshape(KEY_VALUE_HEADS, GROUP, own, HEAD_SIZE)
        return jnp.transpose(a, (2, 0, 1, 3)).reshape(own, nq)

    block = min(512, full)
    scale = 1.0 / math.sqrt(HEAD_SIZE)
    q_heads = to_heads(q)
    empty = jnp.zeros_like(q_heads)
    q_pad = jnp.concatenate([q_heads * jnp.asarray(scale, BF16), empty], axis=-1)
    lo = jnp.tile(my_start, GROUP)[:, None]
    hi = jnp.tile(my_index, GROUP)[:, None]
    span = jnp.stack([my_start[0] // block, my_index[-1] // block + 1]).astype(jnp.int32)
    o_pad, lse = attention_forward(span, q_pad, kv_all, lo, hi, block)
    attended = o_pad[:, :, HEAD_SIZE:]
    attn = from_heads(attended.astype(BF16))

    middle = x_own + dot(attn, w_o, 1, 0)
    inverse_two, normed_two = norm(middle, gain2)
    (normed_two_chip,) = exchange(5, ("col",), [("whole", 1, normed_two)])
    normed_two_chip = normed_two_chip.reshape(chip_len, width)
    gate_up = dot(normed_two_chip, w_pair, 1, 0)
    gate, up = gate_up[:, :half], gate_up[:, half:]
    sig = jax.nn.sigmoid(gate)
    hidden = (gate * sig * up).astype(BF16)
    out_part = dot(hidden, w_down_half, 1, 0).astype(BF16)
    grad_hidden = dot(g_chip, w_down_half, 1, 1)
    grad_gate = grad_hidden * up * sig * (1.0 + gate * (1.0 - sig))
    grad_up = grad_hidden * gate * sig
    grad_pair = jnp.concatenate([grad_gate, grad_up], axis=1).astype(BF16)
    back_part = dot(grad_pair, w_pair, 1, 1).astype(BF16)
    out_parts, back_parts = exchange(
        6,
        ("col",),
        [
            ("block", 1, out_part.reshape(cols, own, width)),
            ("block", 1, back_part.reshape(cols, own, width)),
        ],
    )
    output_own = (middle + total32(out_parts)).astype(BF16)

    gw_pair = dot(normed_two_chip, grad_pair, 0, 0).astype(BF16)
    gw_down = dot(hidden, g_chip, 0, 0).astype(BF16)
    gw_pair = lax.psum_scatter(gw_pair, "row", scatter_dimension=0, tiled=True)
    gw_down = lax.psum_scatter(gw_down, "row", scatter_dimension=1, tiled=True)

    back_two, gg_two = norm_back(middle, gain2, inverse_two, total32(back_parts))
    grad_middle = g_own + back_two
    grad_branch = grad_middle.astype(BF16)
    grad_attn = dot(grad_branch, w_o, 1, 1).astype(BF16)
    do_heads = to_heads(grad_attn)
    delta = jnp.sum(do_heads.astype(F32) * attended, axis=-1, keepdims=True)
    do_pad = jnp.concatenate([empty, do_heads], axis=-1)
    dq_pad, dkv = attention_backward(span, q_pad, do_pad, kv_all, lo, hi, lse, delta, block)

    dkv = dkv.reshape(dps, rows, cols, own, KEY_VALUE_HEADS * 128)
    dkv = jnp.transpose(dkv, (2, 1, 0, 3, 4))
    attn_halves = jnp.transpose(attn.reshape(own, cols, -1), (1, 0, 2))
    dkv_c, attn_c, branch_c = exchange(
        7, ("col",), [("block", 1, dkv), ("block", 1, attn_halves), ("whole", 1, grad_branch)]
    )
    (dkv_r,) = exchange(8, ("row",), [("block", 1, total32(dkv_c).astype(BF16))])
    (dkv_d,) = exchange(9, ("dp",), [("block", 1, total32(dkv_r).astype(BF16))])
    dkv_own = total32(dkv_d).reshape(own, KEY_VALUE_HEADS, 128)
    dq = from_heads(dq_pad[:, :, :HEAD_SIZE]).reshape(own, QUERY_HEADS, HEAD_SIZE) * scale
    dq = rotary(dq, cosine, -sine).astype(BF16).reshape(own, nq)
    dk = rotary(dkv_own[:, :, :HEAD_SIZE], cosine, -sine).astype(BF16).reshape(own, nk)
    dv = dkv_own[:, :, HEAD_SIZE:].astype(BF16).reshape(own, nk)
    grad_qkv = jnp.concatenate([dq, dk, dv], axis=1)
    grad_halves = jnp.concatenate(
        [a.reshape(own, cols, -1) for a in (dq, dk, dv)], axis=2
    )
    (grad_half,) = exchange(
        10, ("col",), [("block", 1, jnp.transpose(grad_halves, (1, 0, 2)))]
    )
    gw_joined = dot(normed_one_chip, grad_half.reshape(chip_len, -1), 0, 0).astype(BF16)
    gw_out = dot(
        branch_c.reshape(chip_len, width), attn_c.reshape(chip_len, -1), 0, 0
    ).astype(BF16)
    back_one, gg_one = norm_back(x_own, gain1, inverse_one, dot(grad_qkv, w_qkv, 1, 1))
    grad_x = grad_middle + back_one

    def by_owner(a):
        return jnp.transpose(a.reshape(own, rows, cols, part), (1, 2, 0, 3))

    gains = jnp.stack([gg_one, gg_two]).reshape(2, rows, cols, part)
    gains = jnp.broadcast_to(jnp.transpose(gains, (1, 2, 0, 3))[:, :, :, None], (rows, cols, 2, 8, part))
    gw_joined, gw_out, output, grad_tokens, gains = exchange(
        11,
        ("row", "col"),
        [
            ("block", 1, gw_joined.reshape(rows, row_block, -1)),
            ("block", 1, gw_out.reshape(rows, row_block, -1)),
            ("block", 2, by_owner(output_own)),
            ("block", 2, by_owner(grad_x)),
            ("block", 2, gains),
        ],
    )
    gw_joined = total32(gw_joined).astype(BF16)
    gw_out = total32(gw_out).astype(BF16)
    gains = jnp.sum(gains, axis=(0, 1))

    def over_dp(a):
        return jnp.transpose(a.reshape(a.shape[0], dps, -1), (1, 0, 2))

    joined = jnp.concatenate(
        [
            over_dp(gw_joined[:, :qc]),
            over_dp(gw_joined[:, qc : qc + kc]),
            over_dp(gw_joined[:, qc + kc :]),
            over_dp(gw_out),
        ],
        axis=2,
    )
    ffn = jnp.concatenate([over_dp(gw_pair[:, :half]), over_dp(gw_pair[:, half:])], axis=2)
    joined, ffn, down, gains = exchange(
        12,
        ("dp",),
        [
            ("block", 1, joined),
            ("block", 1, ffn),
            ("block", 1, gw_down.reshape(dps, half // dps, row_block)),
            ("whole", 1, gains),
        ],
    )
    joined, ffn, down = total32(joined), total32(ffn), total32(down)
    gains = jnp.sum(gains, axis=0)[:, 0]
    qd, kd = qc // dps, kc // dps
    return (
        output.reshape(length, sequences, part),
        grad_tokens.reshape(length, sequences, part),
        gains[0],
        joined[:, :qd],
        joined[:, qd : qd + kd],
        joined[:, qd + kd : qd + 2 * kd],
        joined[:, qd + 2 * kd :].T,
        gains[1],
        ffn[:, : half // dps],
        ffn[:, half // dps :],
        down,
    )


def solution(mesh):
    in_specs = (
        P("dp", None, ("row", "col")),
        P(),
        P(("row", "col")),
        P("row", "col"),
        P("row", "col"),
        P("row", "col"),
        P("col", "row"),
        P(("row", "col")),
        P("row", "col"),
        P("row", "col"),
        P("col", "row"),
        P("dp", None, ("row", "col")),
    )
    out_specs = (
        P("dp", None, ("row", "col")),
        P("dp", None, ("row", "col")),
        P(("row", "col")),
        P("row", ("col", "dp")),
        P("row", ("col", "dp")),
        P("row", ("col", "dp")),
        P(("col", "dp"), "row"),
        P(("row", "col")),
        P("row", ("col", "dp")),
        P("row", ("col", "dp")),
        P(("col", "dp"), "row"),
    )
    return jax.shard_map(shards, mesh=mesh, in_specs=in_specs, out_specs=out_specs, check_vma=False)
```

time: 1480 us -> 780 us (0.53)
  waiting for transfers between devices: 800 us -> 0.77 us
  Pallas kernels: 0 us -> 604 us
  local copies, waits for them, and re-layouts: 300 us -> 73.6 us
  blocking collectives: 115 us -> 0 us
  matrix products: 135 us -> 37.8 us
  loops' own time: 48.1 us -> 0 us
  other arithmetic: 59.3 us -> 38 us
    pallas_call x0 -> x15, Pallas kernels: none -> 604 us  [the longest x13 589 us: exchange(): pl.pallas_call(functools.partial(exchange_kernel, axes, sizes, modes, off...]
    reduce_scatter x15 -> x2, waiting for transfers between devices: 535 us -> 0.01 us  [the longest x1 0.01 us: shards(): gw_down = lax.psum_scatter(gw_down, 'row', scatter_dimension=1, tiled=True)]
    dynamic_update_slice x32 -> x0, local copies, waits for them, and re-layouts: 236 us -> none  [shards(): lax.scan(attend_back, jnp.zeros(queries.shape, jnp.float32), (block_start...]
    all_gather x5 -> x2, waiting for transfers between devices: 221 us -> 0.02 us  [the longest x1 0.02 us: shards(): w_pair = lax.all_gather(pair_block, 'row', axis=0, tiled=True)]
    dot_general x68 -> x12, matrix products: 135 us -> 37.8 us  [dot(): lax.dot_general(a, b, (((ca,), (cb,)), ((), ())), preferred_element_type=...]
    psum x5 -> x0, blocking collectives: 68.3 us -> none  [the longest x4 55.8 us: width_total(): return lax.psum(partial_value, ('row', 'col'))]
    another operation x3 -> x0, loops' own time: 48.1 us -> none  [the longest x1 16.1 us: shards(): lax.scan(attend_back, jnp.zeros(queries.shape, jnp.float32), (block_start...]
    unnamed x24 -> x4, waiting for transfers between devices: 44.4 us -> 0.75 us
  transfers between devices with their start and end apart: 22 -> 4, of which waited for: 21 -> 0; matrix products, arithmetic and copies ran while one was open for 4% -> 16% of each run, Pallas kernels for 0% -> 72%
where the time goes in v1:
time: 780 us; the launch traced here: 772 us
  Pallas kernels  604 us (77%)
  local copies, waits for them, and re-layouts  73.6 us (9%)
  other arithmetic  38 us (5%)
  matrix products  37.8 us (5%)
  between operations  17.5 us (2%)
    pallas_call x13, Pallas kernels, exchange(): pl.pallas_call(functools.partial(exchange_kernel, axes, sizes, modes, off...  589 us
    dot_general x12, matrix products, dot(): lax.dot_general(a, b, (((ca,), (cb,)), ((), ())), preferred_element_type=...  37.8 us
    unnamed x88, local copies, waits for them, and re-layouts  21.7 us
    reduce_sum x10, other arithmetic, total32(): return jnp.sum(a.astype(F32), axis=axis)  17 us
  transfers between devices with their start and end apart: 4, of which 0 were waited for; matrix products, arithmetic and copies ran while one was open for 16% of the time, Pallas kernels for 72%

profile of v1, /device:TPU:0, one launch (start us, length us, event | category | flops | bytes accessed | tf_op | source)
XLA Modules:
  0.0 771.7 jit_solution(7204657443529171332)
XLA Ops:
  7.3 2.6 pad_maximum_fusion.4
  18.0 60.4 %exchange_0.1 = (bf16[4,2,256,120]{3,2,1,0:T(8,128)(2,1)}, bf16[4,2,256,120]{3,2,1,0:T(8,128)(2,1)}, f32[4,2,16,120]{3,2,1,0:T(8,128)}, bf16[4,240,800]{2,1,0:T(8,128)(2,1)}, bf16[4,480,240]{2,1,0:T(8,128)(2,1)}) custom-call(bf16[4,256,120]{2,1,0:T(8,128)(2,1)} %bitcast.181, bf16[4,256,120]{2,1,0:T(8,128)(2,1)} %bitcast.182, ...), custom_call_target="tpu_custom_call" | custom-call | tf_op jit(solution)/shard_map/exchange_0/pallas_call | solution.py:109
  78.4 83.2 %exchange_1.1 = (bf16[2,4,240,800]{3,2,1,0:T(8,128)(2,1)}, bf16[2,4,480,240]{3,2,1,0:T(8,128)(2,1)}) custom-call(bf16[4,240,800]{2,1,0:T(8,128)(2,1)} %get-tuple-element.38.refs_0_, bf16[4,480,240]{2,1,0:T(8,128)(2,1)} %get-tuple-element.39.refs_1_), custom_call_target="tpu_custom_call" | custom-call | tf_op jit(solution)/shard_map/exchange_1/pallas_call | solution.py:109
  161.6 3.2 fusion.22
  165.9 2.1 copy.242
  169.2 2.5 copy.240
  173.0 2.6 convolution_convert_fusion.2
  177.5 16.3 %exchange_2.1.refs_0_ = bf16[4,128,640]{2,1,0:T(8,128)(2,1)} custom-call(bf16[128,640]{1,0:T(8,128)(2,1)} %copy.186.refs_0_), custom_call_target="tpu_custom_call" | custom-call | tf_op jit(solution)/shard_map/exchange_2/pallas_call | solution.py:109
  193.8 31.2 %exchange_3.1.refs_0_ = bf16[4,4,128,640]{3,2,1,0:T(8,128)(2,1)} custom-call(bf16[4,128,640]{2,1,0:T(8,128)(2,1)} %exchange_2.1.refs_0_), custom_call_target="tpu_custom_call" | custom-call | tf_op jit(solution)/shard_map/exchange_3/pallas_call | solution.py:109
  225.0 80.6 %exchange_4.1 = bf16[2,4,4,128,640]{4,3,2,1,0:T(8,128)(2,1)} custom-call(bf16[4,4,128,640]{3,2,1,0:T(8,128)(2,1)} %exchange_3.1.refs_0_), custom_call_target="tpu_custom_call" | custom-call | tf_op jit(solution)/shard_map/exchange_4/pallas_call | solution.py:109
  305.6 5.6 copy.187
  312.0 2.5 copy-done
  314.5 6.0 attend.1
  322.7 4.5 copy.191
  327.2 4.8 reshape.494
  332.1 3.0 multiply_reduce_fusion.5
  335.0 1.9 multiply_convert_fusion.3.refs_0_
  336.9 9.6 %exchange_5.1 = bf16[2,128,960]{2,1,0:T(8,128)(2,1)} custom-call(bf16[128,960]{1,0:T(8,128)(2,1)} %multiply_convert_fusion.3.refs_0_), custom_call_target="tpu_custom_call" | custom-call | tf_op jit(solution)/shard_map/exchange_5/pallas_call | solution.py:109
  347.8 5.7 fusion.27
  353.4 4.9 multiply_convert_fusion.1
  359.2 2.3 convolution_convert_fusion.1
  361.8 5.1 convolution_convert_fusion
  368.2 2.1 fusion.4
  370.2 2.0 copy.176
  373.0 1.8 copy.243
  374.8 1.8 copy.201
  376.6 2.7 convolution_convert_fusion.5
  380.3 4.3 convolution_convert_fusion.4
  385.6 17.0 %exchange_6.1 = (bf16[2,128,960]{2,1,0:T(8,128)(2,1)}, bf16[2,128,960]{2,1,0:T(8,128)(2,1)}) custom-call(bf16[2,128,960]{2,1,0:T(8,128)(2,1)} %bitcast.167, bf16[2,128,960]{2,1,0:T(8,128)(2,1)} %bitcast.168), custom_call_target="tpu_custom_call" | custom-call | tf_op jit(solution)/shard_map/exchange_6/pallas_call | solution.py:109
  408.1 2.0 copy.195
  411.3 1.6 multiply_reduce_fusion
  413.3 8.5 %attend_back.1 = (f32[5,384,128]{2,1,0:T(8,128)S(1)}, bf16[4096,640]{1,0:T(8,128)(2,1)S(1)}) custom-call(s32[2]{0:T(128)S(1)} %pad_add_fusion.span_ref, bf16[5,384,128]{2,1,0:T(8,128)(2,1)S(1)} %concatenate.60.q_ref, bf16[5,384,128]{2,1,0:T(8,128)(2,1)S(1)} %concatenate.64.do_ref, bf16[4096,640]{1,0:T(8,128)(2,1)} %bitcast.138, s32[384,1]{1,0:T(8,128)S(1)} %bitcast.142, ...), custom_call_target="tpu_custom_call" | custom-call | tf_op jit(solution)/shard_map/attend_back/pallas_call | solution.py:215
  421.8 2.8 copy.251
  424.7 93.0 %exchange_7.1 = (bf16[2,4,4,128,640]{4,3,2,1,0:T(8,128)(2,1)}, bf16[2,128,480]{2,1,0:T(8,128)(2,1)}, bf16[2,128,960]{2,1,0:T(8,128)(2,1)}) custom-call(bf16[2,4,4,128,640]{4,3,2,1,0:T(8,128)(2,1)} %bitcast.145, bf16[2,128,480]{2,1,0:T(8,128)(2,1)} %bitcast.179, bf16[128,960]{1,0:T(8,128)(2,1)} %copy-done.10), custom_call_target="tpu_custom_call" | custom-call | tf_op jit(solution)/shard_map/exchange_7/pallas_call | solution.py:109
  517.7 5.8 reduce_sum.218.refs_0_
  523.5 40.2 %exchange_8.1 = bf16[4,4,128,640]{3,2,1,0:T(8,128)(2,1)} custom-call(bf16[4,4,128,640]{3,2,1,0:T(8,128)(2,1)} %reduce_sum.218.refs_0_), custom_call_target="tpu_custom_call" | custom-call | tf_op jit(solution)/shard_map/exchange_8/pallas_call | solution.py:109
  563.7 3.2 reduce_sum.219.refs_0_
  566.9 56.5 %exchange_9.1 = bf16[4,128,640]{2,1,0:T(8,128)(2,1)} custom-call(bf16[4,128,640]{2,1,0:T(8,128)(2,1)} %reduce_sum.219.refs_0_), custom_call_target="tpu_custom_call" | custom-call | tf_op jit(solution)/shard_map/exchange_9/pallas_call | solution.py:109
  626.6 8.1 %exchange_10.1 = bf16[2,128,800]{2,1,0:T(8,128)(2,1)} custom-call(bf16[2,128,800]{2,1,0:T(8,128)(2,1)} %maximum_bitcast_fusion.refs_0_), custom_call_target="tpu_custom_call" | custom-call | tf_op jit(solution)/shard_map/exchange_10/pallas_call | solution.py:109
  634.7 1.7 convolution_convert_fusion.3
  636.4 2.4 copy.206
  640.0 2.8 multiply_reduce_fusion.2
  648.8 42.8 %exchange_11.1 = (bf16[4,240,800]{2,1,0:T(8,128)(2,1)}, bf16[4,240,480]{2,1,0:T(8,128)(2,1)}, bf16[4,2,128,120]{3,2,1,0:T(8,128)(2,1)}, f32[4,2,128,120]{3,2,1,0:T(8,128)}, f32[4,2,2,8,120]{4,3,2,1,0:T(8,128)}) custom-call(bf16[4,240,800]{2,1,0:T(8,128)(2,1)} %bitcast.147, bf16[4,240,480]{2,1,0:T(8,128)(2,1)} %bitcast.154, ...), custom_call_target="tpu_custom_call" | custom-call | tf_op jit(solution)/shard_map/exchange_11/pallas_call | solution.py:109
  691.6 1.9 copy.228
  693.5 2.0 copy.229
  700.8 2.1 copy.227
  705.5 1.5 pad_maximum_fusion.5.refs_1_
  707.0 50.4 %exchange_12.1 = (bf16[4,240,320]{2,1,0:T(8,128)(2,1)}, bf16[4,240,640]{2,1,0:T(8,128)(2,1)}, bf16[4,320,240]{2,1,0:T(8,128)(2,1)}, f32[4,2,8,120]{3,2,1,0:T(8,128)}) custom-call(bf16[4,240,320]{2,1,0:T(8,128)(2,1)} %pad_maximum_fusion.8.refs_0_, bf16[4,240,640]{2,1,0:T(8,128)(2,1)} %pad_maximum_fusion.5.refs_1_, bf16[4,320,240]{2,1,0:T(8,128)(2,1)} %bitcast.158, ...), custom_call_target="tpu_custom_call" | custom-call | tf_op jit(solution)/shard_map/exchange_12/pallas_call | solution.py:109
  (196 shorter events, 52.9 us)
Async XLA Ops:
  7.2 3.5 copy-start.29
  7.2 7.4 copy-start.24
  7.2 8.2 %copy-start.25 = (bf16[1024,1,120]{0,2,1:T(8,128)(2,1)S(1)}, bf16[1024,1,120]{0,2,1:T(8,128)(2,1)}, u32[]{:S(2)}) copy-start(bf16[1024,1,120]{0,2,1:T(8,128)(2,1)} %param.23) | copy-start | bytes 737284
  7.2 340.5 %all-gather.3.cloned.1.call-start = ((), (), s32[]{:S(2)}) async-start(), calls=%async_computation.2 | async-start | bytes 6144000 | tf_op jit(solution)/shard_map/all_gather | solution.py:276
  9.8 6.4 copy-start.26
  9.8 6.5 copy-start.27
  9.8 6.6 copy-start.31
  9.8 6.7 copy-start.32
  9.8 7.3 copy-start.23
  9.9 343.5 %all-gather.5.cloned.1.call-start = ((), (), s32[]{:S(2)}) async-start(), calls=%async_computation.3 | async-start | bytes 3072000 | tf_op jit(solution)/shard_map/all_gather | solution.py:277
  10.6 690.2 %reduce-scatter.5.cloned.1.call-start = ((), (), s32[]{:S(2)}) async-start(), calls=%async_computation.5 | async-start | bytes 3072000 | tf_op jit(solution)/shard_map/reduce_scatter | solution.py:381
  161.6 3.2 copy-start.9
  169.2 2.5 copy-start.8
  171.7 1.1 copy-start.16
  171.8 1.3 copy-start.18
  172.4 3.7 copy-start.4
  312.0 2.5 copy-start
  322.7 9.4 %copy-start.12 = (bf16[5,3,128,64]{2,3,1,0:T(8,128)(2,1)}, bf16[5,3,128,64]{2,3,1,0:T(8,128)(2,1)S(1)}, u32[]{:S(2)}) copy-start(bf16[5,3,128,64]{2,3,1,0:T(8,128)(2,1)S(1)} %copy.190) | copy-start | bytes 737284
  358.3 0.9 copy-start.19
  361.5 341.5 %reduce-scatter.3.cloned.1.call-start = ((), (), s32[]{:S(2)}) async-start(), calls=%async_computation.4 | async-start | bytes 6144000 | tf_op jit(solution)/shard_map/reduce_scatter | solution.py:380
  402.6 4.1 copy-start.3
  404.0 4.1 copy-start.6
  406.7 3.3 copy-start.10
  421.8 2.9 copy-start.1
  566.9 58.2 %copy-start.2 = (f32[5,384,128]{2,1,0:T(8,128)S(1)}, f32[5,384,128]{2,1,0:T(8,128)}, u32[]{:S(2)}) copy-start(f32[5,384,128]{2,1,0:T(8,128)} %copy-done.1) | copy-start | bytes 2949124
  625.4 9.3 %copy-start.13 = (bf16[256,4,2,120]{0,3,2,1:T(8,128)(2,1)S(1)}, bf16[256,4,2,120]{0,3,2,1:T(8,128)(2,1)}, u32[]{:S(2)}) copy-start(bf16[256,4,2,120]{0,3,2,1:T(8,128)(2,1)} %copy.176) | copy-start | bytes 1474564
  636.4 3.6 copy-start.5
  636.4 3.6 copy-start.17
  640.0 2.9 copy-start.7
  640.0 2.9 copy-start.11
  644.2 2.5 copy-start.21
  644.3 2.5 copy-start.22
  691.6 5.7 copy-start.14
  697.8 1.0 copy-start.28
  757.4 2.2 copy-start.30
  757.4 4.9 copy-start.15
  762.3 2.1 copy-start.20
Sparse Core Ops, SparseCore 0:
  10.0 94.3 all-gather.2
  106.2 38.5 all-gather.4
  361.6 60.8 reduce-scatter.4
  425.4 58.7 reduce-scatter.2
